TPU v7x, 256 devices: a whole 4x4x8 slice. The times are simulated.
256 devices in a mesh: ctx: 32 (over x_lo, z, core), tp: 8 (over x_hi, y).
Axes of the slice: x: 4 (x_hi: 2, x_lo: 2; x = x_hi * 2 + x_lo), y: 4, z: 8, core: 2. Of those that a mesh axis runs over, the one named last changes fastest.
Arguments:
- prompt_x: bfloat16 [2048, 5120], P('ctx', 'tp'), may hold values from -6 to 6
- resp_x: bfloat16 [2048, 5120], P('ctx', 'tp'), may hold values from -6 to 6
- span_ids: int32 [64], replicated, may hold values from 0 to 63, each once
- lengths: int32 [16], replicated, may hold values from 16 to 128, as said below
- in_gain: float32 [5120], replicated, may hold values from 0.5 to 2
- q_gain: float32 [128], replicated, may hold values from 0.5 to 6, as said below
- k_gain: float32 [128], replicated, may hold values from 0.5 to 6, as said below
- w_query: bfloat16 [5120, 8192], P('ctx', 'tp'), may hold values from -0.078125 to 0.078125
- w_keyval: bfloat16 [5120, 2, 1024], P('ctx', None, 'tp'), may hold values from -0.078125 to 0.078125
- w_out: bfloat16 [8192, 5120], P('tp', 'ctx'), may hold values from -1 to 1
Outputs:
- prompt_out: bfloat16 [2048, 5120], P('ctx', 'tp')
- resp_out: bfloat16 [2048, 5120], P('ctx', 'tp')
Inputs may be any that keep to these rules, and one draw needn't show every extreme that they name: `lengths`: one response has length 128 and one has 16. `q_gain`: positive. `k_gain`: positive.
All inputs are finite; a program needn't handle non-finite values.
Results may differ from a plain program's by a relative error of at most 0.02.
The roundings to bfloat16 on the way count: a program that leaves them out, or rounds other values in their place, can miss the bound.
Values may be sent and summed in bfloat16 or wider, within the bound.
A program may use at most 128 MiB of HBM per device.

v0:
```python
import jax
import jax.numpy as jnp
from jax import lax
from jax.sharding import PartitionSpec as P


def shifted(shard, axis, by):
    length = lax.axis_size(axis)
    pairs = [(i, i + by) for i in range(length) if 0 <= i + by < length]
    return lax.ppermute(shard, axis, pairs)


def head_norm(values, gain):
    return values * lax.rsqrt(jnp.mean(values * values, axis=-1, keepdims=True) + 1e-06) * gain


def rotary(values, positions):
    half_dim = values.shape[-1] // 2
    inverse = 1000000.0 ** (-(jnp.arange(half_dim, dtype=jnp.float32) * 2.0) / values.shape[-1])
    angles = positions.astype(jnp.float32)[:, None] * inverse[None, :]
    cosine = jnp.concatenate([jnp.cos(angles), jnp.cos(angles)], axis=-1)[:, None, :]
    sine = jnp.concatenate([jnp.sin(angles), jnp.sin(angles)], axis=-1)[:, None, :]
    rotated = jnp.concatenate([-values[..., half_dim:], values[..., :half_dim]], axis=-1)
    return values * cosine + rotated * sine


def span_positions(table, first_row, count, span_rows):
    global_rows = first_row + jnp.arange(count, dtype=jnp.int32)
    owners = global_rows // span_rows
    matches = owners[:, None] == jnp.arange(table.shape[0], dtype=jnp.int32)[None, :]
    return (
        jnp.sum(jnp.where(matches, table[None, :], 0), axis=1) * span_rows + global_rows % span_rows
    )


def fresh_state(kv_heads, group, count, head_dim):
    return (
        jnp.full((kv_heads, group, count), -1e30, jnp.float32),
        jnp.zeros((kv_heads, group, count), jnp.float32),
        jnp.zeros((kv_heads, group, count, head_dim), jnp.float32),
    )


def softmax_update(state, queries, keys, values, allowed):
    old_peak, old_total, old_accum = state
    scale = queries.shape[-1] ** (-0.5)
    scores = jnp.einsum("qhgd,khd->hgqk", queries, keys, preferred_element_type=jnp.float32) * scale
    masked = jnp.where(allowed[None, None], scores, -1e30)
    new_peak = jnp.maximum(old_peak, jnp.max(masked, axis=-1))
    weights = jnp.where(allowed[None, None], jnp.exp(scores - new_peak[..., None]), 0.0)
    factor = jnp.exp(old_peak - new_peak)
    new_total = old_total * factor + jnp.sum(weights, axis=-1)
    product = jnp.einsum(
        "hgqk,khd->hgqd", weights.astype(jnp.bfloat16), values, preferred_element_type=jnp.float32
    )
    return (new_peak, new_total, old_accum * factor[..., None] + product)


def blocked_update(state, queries, keys, values, allowed):
    count = keys.shape[0]
    block_cols = 512
    for begin in range(0, count, block_cols):
        end = min(count, begin + block_cols)
        state = softmax_update(
            state, queries, keys[begin:end], values[begin:end], allowed[:, begin:end]
        )
    return state


def finish(state):
    peak_unused, total, accum = state
    scaled = accum / total[..., None]
    count = scaled.shape[2]
    return jnp.transpose(scaled, (2, 0, 1, 3)).reshape(count, -1).astype(jnp.bfloat16)


def body(prompt_x, resp_x, span_ids, lengths, in_gain, q_gain, k_gain, w_query, w_keyval, w_out):
    prompt_full, resp_full = (
        lax.all_gather(prompt_x, "tp", axis=1, tiled=True),
        lax.all_gather(resp_x, "tp", axis=1, tiled=True),
    )
    prompt_rows = prompt_full.shape[0]
    resp_rows = resp_full.shape[0]
    ctx_count = lax.axis_size("ctx")
    ctx_index = lax.axis_index("ctx")
    span_rows = prompt_rows // (span_ids.shape[0] // ctx_count)
    all_rows = prompt_rows + resp_rows
    head_dim = q_gain.shape[0]
    kv_heads = w_keyval.shape[2] // head_dim
    q_heads = w_query.shape[1] // head_dim
    group = q_heads // kv_heads
    joined = jnp.concatenate([prompt_full, resp_full], axis=0).astype(jnp.float32)
    normed = head_norm(joined, in_gain).astype(jnp.bfloat16)
    query_w, keyval_w, out_w = (
        lax.all_gather(w_query, "ctx", axis=0, tiled=True),
        lax.all_gather(w_keyval, "ctx", axis=0, tiled=True),
        lax.all_gather(w_out, "ctx", axis=1, tiled=True),
    )
    query = jnp.dot(normed, query_w, preferred_element_type=jnp.float32)
    keyval = jnp.dot(
        normed, keyval_w.reshape(keyval_w.shape[0], -1), preferred_element_type=jnp.float32
    )
    half_index = ctx_index % 2
    prompt_pos = span_positions(span_ids, ctx_index * prompt_rows, prompt_rows, span_rows)
    resp_pos = (
        prompt_rows * ctx_count + half_index * resp_rows + jnp.arange(resp_rows, dtype=jnp.int32)
    )
    positions = jnp.concatenate([prompt_pos, resp_pos])
    keyval = keyval.reshape(all_rows, 2, kv_heads, head_dim)
    queries = rotary(
        head_norm(query.reshape(all_rows, q_heads, head_dim), q_gain), positions
    ).astype(jnp.bfloat16)
    queries = queries.reshape(all_rows, kv_heads, group, head_dim)
    keys = rotary(head_norm(keyval[:, 0], k_gain), positions).astype(jnp.bfloat16)
    values = keyval[:, 1].astype(jnp.bfloat16)
    prompt_q, resp_q = (queries[:prompt_rows], queries[prompt_rows:])
    prompt_k, resp_k = (keys[:prompt_rows], keys[prompt_rows:])
    prompt_v, resp_v = (values[:prompt_rows], values[prompt_rows:])
    piece_k = lax.all_gather(prompt_k, "ctx", axis=0, tiled=True)
    count = piece_k.shape[0]
    key_pos = span_positions(span_ids, jnp.int32(0), count, span_rows)
    allowed = key_pos[None, :] <= prompt_pos[:, None]
    prompt_state = blocked_update(
        fresh_state(kv_heads, group, prompt_rows, head_dim),
        prompt_q,
        piece_k,
        lax.all_gather(prompt_v, "ctx", axis=0, tiled=True),
        allowed,
    )
    every_k, every_v = (
        lax.all_gather(prompt_k, "ctx", axis=0, tiled=True),
        lax.all_gather(prompt_v, "ctx", axis=0, tiled=True),
    )
    resp_state = blocked_update(
        fresh_state(kv_heads, group, resp_rows, head_dim),
        resp_q,
        every_k,
        every_v,
        jnp.ones((resp_rows, every_k.shape[0]), bool),
    )
    lower_k, lower_v = shifted((resp_k, resp_v), "ctx", 1)
    offsets = jnp.arange(resp_rows, dtype=jnp.int32)
    own_allowed = jnp.concatenate(
        [
            jnp.broadcast_to(half_index == 1, (resp_rows, resp_rows)),
            offsets[None, :] <= offsets[:, None],
        ],
        axis=1,
    )
    resp_state = blocked_update(
        resp_state,
        resp_q,
        jnp.concatenate([lower_k, resp_k]),
        jnp.concatenate([lower_v, resp_v]),
        own_allowed,
    )
    attended = jnp.concatenate([finish(prompt_state), finish(resp_state)], axis=0)
    projected = jnp.dot(attended, out_w, preferred_element_type=jnp.float32)
    resp_length = lengths[ctx_index // 2]
    keep = jnp.concatenate(
        [jnp.ones((prompt_rows,), bool), half_index * resp_rows + offsets < resp_length]
    )
    projected = jnp.where(keep[:, None], projected, 0.0)
    summed = lax.psum_scatter(projected.astype(jnp.bfloat16), "tp", scatter_dimension=1, tiled=True)
    return (summed[:prompt_rows], summed[prompt_rows:])


def solution(mesh):
    placed = (
        P("ctx", "tp"),
        P("ctx", "tp"),
        P(),
        P(),
        P(),
        P(),
        P(),
        P("ctx", "tp"),
        P("ctx", None, "tp"),
        P("tp", "ctx"),
    )
    return jax.shard_map(
        body,
        mesh=mesh,
        in_specs=placed,
        out_specs=(P("ctx", "tp"), P("ctx", "tp")),
        check_vma=False,
    )
```

profile of v0, /device:TPU:16, one launch (start us, length us, event | category | flops | bytes accessed | tf_op | source)
XLA Modules:
  0.0 327.4 jit_solution(15900187262418692412)
XLA Ops:
  7.2 0.7 all-gather.5.cloned.1.call-update
  8.0 0.7 all-gather.7.cloned.1.call-update
  8.7 0.7 all-gather.9.cloned.1.call-update
  9.6 1.2 dynamic_slice.3
  10.8 0.7 add_compare_fusion
  11.5 34.1 %all_gather.23 = bf16[64,5120]{1,0:T(8,128)(2,1)S(1)} all-gather(bf16[64,640]{1,0:T(8,128)(2,1)} %param.10), channel_id=1, replica_groups=mesh['ctx'=32,'tp'=8] {'tp'}, dimensions={1}, use_global_device_ids=true | all-gather | bytes 737280 | tf_op jit(solution)/shard_map/all_gather | solution.py:79
  45.6 38.5 %all_gather.24 = bf16[64,5120]{1,0:T(8,128)(2,1)} all-gather(bf16[64,640]{1,0:T(8,128)(2,1)} %param.11), channel_id=1, replica_groups=mesh['ctx'=32,'tp'=8] {'tp'}, dimensions={1}, use_global_device_ids=true | all-gather | bytes 737280 | tf_op jit(solution)/shard_map/all_gather | solution.py:80
  84.1 1.4 fusion.1
  85.8 1.0 multiply_cosine_fusion
  87.4 5.9 %copy.33 = bf16[5120,2,128]{0,2,1:T(8,128)(2,1)S(1)} copy(bf16[5120,2,128]{2,1,0:T(2,128)(2,1)} %all-gather.5.cloned.1.call-done) | data formatting | bytes 5242880 | tf_op jit(solution)/shard_map/reshape | solution.py:101
  93.4 2.2 fusion.145
  96.0 1.3 collective-permute-start
  97.3 3.3 %collective-permute-start.1 = (bf16[64,1,128]{2,0,1:T(8,128)(2,1)S(1)}, bf16[64,1,128]{2,0,1:T(8,128)(2,1)S(1)}, u32[]{:S(2)}, u32[]{:S(2)}) collective-permute-start(bf16[64,1,128]{2,0,1:T(8,128)(2,1)S(1)} %get-tuple-element.26), channel_id=1, source_target_pairs={{0,8},{8,16},{16,24},{24,32},{32,40},{40,48},{48,56},{56,64},{64,7... | collective-permute-start | bytes 49160 | tf_op jit(solution)/shard_map/ppermute | solution.py:10
  100.7 37.4 %all_gather.26 = bf16[2048,1,128]{2,0,1:T(8,128)(2,1)S(1)} all-gather(bf16[64,1,128]{2,0,1:T(8,128)(2,1)S(1)} %get-tuple-element.31), channel_id=1, replica_groups=mesh['ctx'=32,'tp'=8] {'ctx'}, dimensions={0}, use_global_device_ids=true | all-gather | bytes 540672 | tf_op jit(solution)/shard_map/all_gather | solution.py:119
  138.0 32.6 %all-gather = bf16[2048,1,1,128]{3,0,1,2:T(8,128)(2,1)S(1)} all-gather(bf16[64,1,1,128]{3,0,1,2:T(8,128)(2,1)S(1)} %get-tuple-element.27), channel_id=2, replica_groups=mesh['ctx'=32,'tp'=8] {'ctx'}, dimensions={0}, use_global_device_ids=true | all-gather | bytes 540672 | tf_op jit(solution)/shard_map/all_gather | solution.py:127
  170.6 5.8 %fusion.131 = f32[128,1024]{1,0:T(8,128)S(1)} fusion(bf16[5120,1024]{1,0:T(8,128)(2,1)} %all-gather.7.cloned.1.call-done, f32[5120]{0:T(1024)} %param.14, f32[128]{0:T(128)S(1)} %add_rsqrt_fusion.2, bf16[64,5120]{1,0:T(8,128)(2,1)} %all_gather.24, bf16[64,5120]{1,0:T(8,128)(2,1)S(1)} %all_gather.23), kind=kOutput, calls=%fused_computation.217 | convolution fusion | flops 1346764800 | bytes 12341760 | tf_op jit(solution)/shard_map/dot_general | solution.py:99
  180.2 0.4 select_reduce_fusion.1
  187.7 45.0 %all-gather.9.cloned.1.call-done = bf16[1024,5120]{0,1:T(8,128)(2,1)} async-done(((bf16[1024,160]{0,1:T(8,128)(2,1)}), bf16[1024,5120]{0,1:T(8,128)(2,1)}) %all-gather.9.cloned.1.call-update) | async-done | bytes 10485776 | tf_op jit(solution)/shard_map/all_gather | solution.py:97
  232.7 7.5 %fusion = bf16[128,5120]{1,0:T(8,128)(2,1)S(1)} fusion(bf16[1024,5120]{0,1:T(8,128)(2,1)} %all-gather.9.cloned.1.call-done, pred[128]{0:T(512)(128)(4,1)S(1)} %concatenate.69, bf16[64,1024]{1,0:T(8,128)(2,1)S(1)} %bitcast.210, bf16[64,1024]{1,0:T(8,128)(2,1)S(1)} %bitcast.209), kind=kOutput, calls=%fused_computation.1 | convolution fusion | flops 1344012288 | bytes 12058752 | tf_op jit(solution)/shard_map/dot_general | solution.py:158
  240.3 1.5 copy.34
  241.8 76.4 %reduce-scatter.4.cloned.1.call-done = bf16[640,128]{1,0:T(8,128)(2,1)} async-done(((bf16[5120,128]{1,0:T(8,128)(2,1)}), bf16[640,128]{1,0:T(8,128)(2,1)}) %reduce-scatter.4.cloned.1.call-update) | async-done | bytes 163856
  318.2 1.1 fusion.138
  319.3 0.8 copy.36
  320.1 0.8 copy.37
  (83 shorter events, 12.2 us)
Async XLA Ops:
  7.2 78.4 %copy-start.4 = (s32[64]{0:T(128)S(1)}, s32[64]{0:T(128)}, u32[]{:S(2)}) copy-start(s32[64]{0:T(128)} %param.12) | copy-start | bytes 772
  7.2 80.2 %all-gather.5.cloned.1.call-start = ((), (), s32[]{:S(2)}) async-start(), calls=%async_computation.1 | async-start | bytes 2703360 | tf_op jit(solution)/shard_map/all_gather | solution.py:96
  7.9 162.7 %all-gather.7.cloned.1.call-start = ((), (), s32[]{:S(2)}) async-start(), calls=%async_computation.2 | async-start | bytes 10813440 | tf_op jit(solution)/shard_map/all_gather | solution.py:95
  8.7 224.1 %all-gather.9.cloned.1.call-start = ((), (), s32[]{:S(2)}) async-start(), calls=%async_computation.3 | async-start | bytes 10813440 | tf_op jit(solution)/shard_map/all_gather | solution.py:97
  9.4 308.8 %reduce-scatter.4.cloned.1.call-start = ((), (), s32[]{:S(2)}) async-start(), calls=%async_computation.4 | async-start | bytes 1474560
  93.3 2.3 copy-start.2
  93.3 2.5 copy-start
  93.4 2.5 copy-start.1
  96.0 81.6 %collective-permute-start = (bf16[64,1,128]{2,0,1:T(8,128)(2,1)S(1)}, bf16[64,1,128]{2,0,1:T(8,128)(2,1)S(1)}, u32[]{:S(2)}, u32[]{:S(2)}) collective-permute-start(bf16[64,1,128]{2,0,1:T(8,128)(2,1)S(1)} %get-tuple-element.30), channel_id=1, source_target_pairs={{0,8},{8,16},{16,24},{24,32},{32,40},{40,48},{48,56},{56,64},{64,7... | collective-permute-start | bytes 49160 | tf_op jit(solution)/shard_map/ppermute | solution.py:10
  97.3 90.0 %collective-permute-start.1 = (bf16[64,1,128]{2,0,1:T(8,128)(2,1)S(1)}, bf16[64,1,128]{2,0,1:T(8,128)(2,1)S(1)}, u32[]{:S(2)}, u32[]{:S(2)}) collective-permute-start(bf16[64,1,128]{2,0,1:T(8,128)(2,1)S(1)} %get-tuple-element.26), channel_id=1, source_target_pairs={{0,8},{8,16},{16,24},{24,32},{32,40},{40,48},{48,56},{56,64},{64,7... | collective-permute-start | bytes 49160 | tf_op jit(solution)/shard_map/ppermute | solution.py:10
  170.6 6.2 %copy-start.3 = (f32[128]{0:T(128)S(1)}, f32[128]{0:T(128)}, u32[]{:S(2)}) copy-start(f32[128]{0:T(128)} %param.15) | copy-start | bytes 1540
Sparse Core Ops, SparseCore 0:
  9.9 68.2 all-gather.4
  80.0 76.7 all-gather.6
  158.7 74.0 all-gather.8
  241.9 76.2 reduce-scatter.3
where the time goes:
time: 329 us; the launch traced here: 327 us
  blocking collectives  143 us (43%)
  waiting for transfers between devices  124 us (38%)
  matrix products  22 us (7%)
  between operations  14.3 us (4%)
  local copies, waits for them, and re-layouts  11.8 us (4%)
  other arithmetic  8.4 us (3%)
  starting transfers between devices  4.76 us (1%)
    unnamed x5, waiting for transfers between devices  78.5 us
    all_gather x1, waiting for transfers between devices, body(): lax.all_gather(w_out, 'ctx', axis=1, tiled=True)  45 us
    all_gather x1, blocking collectives, body(): lax.all_gather(resp_x, 'tp', axis=1, tiled=True)  38.5 us
    all_gather x1, blocking collectives, body(): piece_k = lax.all_gather(prompt_k, 'ctx', axis=0, tiled=True)  37.4 us
    all_gather x1, blocking collectives, body(): lax.all_gather(prompt_x, 'tp', axis=1, tiled=True)  34.1 us
    all_gather x1, blocking collectives, body(): lax.all_gather(prompt_v, 'ctx', axis=0, tiled=True)  32.6 us
    dot_general x1, matrix products, body(): projected = jnp.dot(attended, out_w, preferred_element_type=jnp.float32)  7.54 us
  transfers between devices with their start and end apart: 6, of which 2 were waited for; matrix products, arithmetic and copies ran while one was open for 9% of the time, Pallas kernels for 0%

commit v1 on v0

v1 whole, which is shorter than its diff:
```python
import functools

import jax
import jax.numpy as jnp
import numpy as np
from jax import lax
from jax.experimental import pallas as pl
from jax.experimental.pallas import tpu as pltpu
from jax.sharding import PartitionSpec as P

MESH = pl.DeviceIdType.MESH
BF = jnp.bfloat16
F32 = jnp.float32
NT = (((1,), (1,)), ((), ()))


def remote(src, dst, send, recv, dev):
    return pltpu.make_async_remote_copy(
        src_ref=src, dst_ref=dst, send_sem=send, recv_sem=recv, device_id=dev, device_id_type=MESH
    )


class Ring:
    def __init__(self, view, send, recv, z, up_dev, down_dev, parts=2):
        self.view, self.send, self.recv, self.z, self.parts = view, send, recv, z, parts
        self.devs = (up_dev, down_dev)

    def items(self, step):
        every = [(way, part) for part in range(self.parts) for way in (0, 1)]
        return every if step < 3 else [i for i in every if i[0] == i[1] * 2 // self.parts]

    def block(self, way, step):
        return lax.rem(self.z + (8 - step if way == 0 else step), 8)

    def copy(self, way, step, part, src=None):
        there = self.view(self.block(way, step), part)
        return remote(
            there if src is None else src, there,
            self.send.at[way, step, part], self.recv.at[way, step, part], self.devs[way],
        )

    def arrived(self, way, step, part):
        here = self.view(self.block(way, step + 1), part)
        remote(
            here, here, self.send.at[way, step, part], self.recv.at[way, step, part],
            self.devs[way],
        ).wait_recv()

    def start(self, part, src=None):
        for way in (0, 1):
            self.copy(way, 0, part, src).start()

    def forward(self, step, then=None, parts=None):
        for way, part in self.items(step - 1):
            if parts is not None and part not in parts:
                continue
            self.arrived(way, step - 1, part)
            if step < 4 and (way, part) in self.items(step):
                self.copy(way, step, part).start()
            if then is not None:
                then(way, step - 1, part)

    def last(self, then=None):
        self.forward(4, then)

    def drain(self):
        for step in range(4):
            for way, part in self.items(step):
                self.copy(way, step, part).wait_send()


class Plane:
    def __init__(self, view, src, a, b, a_dev, b_dev, sems):
        self.view, self.src, self.a, self.b = view, src, a, b
        self.a_dev, self.b_dev = a_dev, b_dev
        self.sa, self.ra, self.sb, self.rb = sems
        self.drains = []

    def go(self, src, dst, send, recv, to):
        make = lambda: remote(src, dst, send, recv, to)
        make().start()
        self.drains.append(lambda: make().wait_send())

    def wait(self, dst, recv, to):
        remote(dst, dst, recv, recv, to).wait_recv()

    def near(self, at, way):
        return (at + (1 if way == 0 else 3)) % 4

    def entry(self, j):
        at = [self.a, self.near(self.a, 1), self.near(self.a, 0)] + [(self.a + 2) % 4] * 2
        return at[j], (None if j < 3 else j - 3)

    def send_a(self):
        own = self.view(self.a, self.b)
        for way in (0, 1):
            self.go(
                self.src, own, self.sa.at[0, way], self.ra.at[0, way],
                self.a_dev(self.near(self.a, way)),
            )

    def send_b(self, j, src=None):
        at, half = self.entry(j)
        part = self.view(at, self.b, half)
        for way in (0, 1):
            self.go(
                part if src is None else src, part, self.sb.at[0, way, j], self.rb.at[0, way, j],
                self.b_dev(self.near(self.b, way)),
            )

    def pass_a(self):
        for way in (0, 1):
            at = self.near(self.a, 1 - way)
            self.wait(self.view(at, self.b), self.ra.at[0, way], self.a_dev(at))
            half = self.view(at, self.b, way)
            self.go(
                half, half, self.sa.at[1, way], self.ra.at[1, way],
                self.a_dev(self.near(self.a, way)),
            )
            self.send_b(1 + way)

    def pass_far(self):
        far = (self.a + 2) % 4
        for way in (0, 1):
            self.wait(self.view(far, self.b, way), self.ra.at[1, way], self.a_dev(far))
            self.send_b(3 + way)

    def pass_b(self, j):
        at, half = self.entry(j)
        for way in (0, 1):
            near = self.near(self.b, 1 - way)
            self.wait(self.view(at, near, half), self.rb.at[0, way, j], self.b_dev(near))
            if half is None or half == way:
                part = self.view(at, near, way)
                self.go(
                    part, part, self.sb.at[1, way, j], self.rb.at[1, way, j],
                    self.b_dev(self.near(self.b, way)),
                )

    def end_b(self, j):
        at, half = self.entry(j)
        far = (self.b + 2) % 4
        for way in (0, 1):
            if half is None or half == way:
                self.wait(self.view(at, far, way), self.rb.at[1, way, j], self.b_dev(far))


class Spread:
    def __init__(self, view, other, sems, z, to_z, twin):
        self.view, self.other, self.z, self.to_z, self.twin = view, other, z, to_z, twin
        self.send, self.recv, self.tsend, self.trecv = sems

    def make(self, way, k, sender):
        sign = 1 if way == 0 else -1
        hops, owner = ((1, 0), (2, 0), (1, 2), (2, 2))[k]
        start = self.z if sender else self.z - sign * hops
        block = (start - sign * owner + 16) % 8
        part = self.view(block, way if k == 3 else None)
        return remote(
            part, part, self.send.at[way, k], self.recv.at[way, k],
            self.to_z((self.z + sign * hops + 8) % 8),
        )

    def pair(self, way, k, view):
        sign = 1 if way == 0 else -1
        block = (self.z - sign * (k + 1) + 16) % 8
        part = view(block, way if k == 3 else None)
        return remote(part, part, self.tsend.at[way, k], self.trecv.at[way, k], self.twin)

    def start(self):
        for k in (1, 0):
            for way in (0, 1):
                self.make(way, k, True).start()

    def arrive(self, way, k):
        self.make(way, k, False).wait_recv()
        self.pair(way, k, self.view).start()

    def middle(self):
        for way in (0, 1):
            self.arrive(way, 1)
            self.make(way, 3, True).start()
            self.make(way, 2, True).start()
        for way in (0, 1):
            self.arrive(way, 0)

    def last(self):
        for k in (3, 2):
            for way in (0, 1):
                self.arrive(way, k)

    def twins(self):
        for k in range(4):
            for way in (0, 1):
                self.pair(way, k, self.other).wait_recv()

    def drain(self):
        for k in range(4):
            for way in (0, 1):
                self.make(way, k, True).wait_send()
                self.pair(way, k, self.view).wait_send()


class Plane:
    def __init__(self, view, src, a, b, a_dev, b_dev, sems):
        self.view, self.src, self.a, self.b = view, src, a, b
        self.a_dev, self.b_dev = a_dev, b_dev
        self.sa, self.ra, self.sb, self.rb = sems
        self.drains = []

    def go(self, src, dst, send, recv, to):
        make = lambda: remote(src, dst, send, recv, to)
        make().start()
        self.drains.append(lambda: make().wait_send())

    def wait(self, dst, recv, to):
        remote(dst, dst, recv, recv, to).wait_recv()

    def near(self, at, way):
        return (at + (1 if way == 0 else 3)) % 4

    def entry(self, j):
        at = [self.a, self.near(self.a, 1), self.near(self.a, 0)] + [(self.a + 2) % 4] * 2
        return at[j], (None if j < 3 else j - 3)

    def send_a(self):
        own = self.view(self.a, self.b)
        for way in (0, 1):
            self.go(
                self.src, own, self.sa.at[0, way], self.ra.at[0, way],
                self.a_dev(self.near(self.a, way)),
            )

    def send_b(self, j, src=None):
        at, half = self.entry(j)
        part = self.view(at, self.b, half)
        for way in (0, 1):
            self.go(
                part if src is None else src, part, self.sb.at[0, way, j], self.rb.at[0, way, j],
                self.b_dev(self.near(self.b, way)),
            )

    def pass_a(self):
        for way in (0, 1):
            at = self.near(self.a, 1 - way)
            self.wait(self.view(at, self.b), self.ra.at[0, way], self.a_dev(at))
            half = self.view(at, self.b, way)
            self.go(
                half, half, self.sa.at[1, way], self.ra.at[1, way],
                self.a_dev(self.near(self.a, way)),
            )
            self.send_b(1 + way)

    def pass_far(self):
        far = (self.a + 2) % 4
        for way in (0, 1):
            self.wait(self.view(far, self.b, way), self.ra.at[1, way], self.a_dev(far))
            self.send_b(3 + way)

    def pass_b(self, j):
        at, half = self.entry(j)
        for way in (0, 1):
            near = self.near(self.b, 1 - way)
            self.wait(self.view(at, near, half), self.rb.at[0, way, j], self.b_dev(near))
            if half is None or half == way:
                part = self.view(at, near, way)
                self.go(
                    part, part, self.sb.at[1, way, j], self.rb.at[1, way, j],
                    self.b_dev(self.near(self.b, way)),
                )

    def end_b(self, j):
        at, half = self.entry(j)
        far = (self.b + 2) % 4
        for way in (0, 1):
            if half is None or half == way:
                self.wait(self.view(at, far, way), self.rb.at[1, way, j], self.b_dev(far))


class Twin:
    def __init__(self, ring, other, send, recv, dev):
        self.ring, self.other, self.sems, self.dev = ring, other, (send, recv), dev

    def make(self, way, step, half, view):
        part = view(self.ring.block(way, step + 1), half)
        return remote(
            part, part, self.sems[0].at[way, step, half], self.sems[1].at[way, step, half], self.dev
        )

    def __call__(self, way, step, half):
        self.make(way, step, half, self.ring.view).start()

    def each(self, steps):
        return [(way, step, half) for step in steps for way, half in self.ring.items(step)]

    def wait_recv(self, steps):
        for item in self.each(steps):
            self.make(*item, self.other).wait_recv()

    def drain(self):
        for item in self.each(range(4)):
            self.make(*item, self.ring.view).wait_send()


def rows_of(start, size, unit):
    return pl.ds(pl.multiple_of(start, unit), size)


def kernel(
    spans, lens, px, rx, gain, qg, kg, inv, wq, wkv, wo,
    po, ro,
    xr, nb, wqb, wkb, wob, wkl, accq, acck, cosb, sinb, rpos, kpos, qb, kvp, kvr, atts, attb,
    osend, ry, xs, xrx,
    loc, xas, xar, xbs, xbr, gs, gr, ks, kr, qrs, qrr, krs, krr, ors, orr, ots, otr, o1,
    nbs, nbr, kvs, kvrv, vrs, vrr, vts, vtr, ats, atr, ys, yr, zs, zr,
):
    ctx, tp = lax.axis_index("ctx"), lax.axis_index("tp")
    low, z, c = ctx // 16, (ctx // 2) % 8, ctx % 2
    hi, y = tp // 4, tp % 4
    x = hi * 2 + low
    olow, oc = 1 - low, 1 - c

    def dev(low_, z_, c_, hi_, y_):
        return (low_ * 16 + z_ * 2 + c_, hi_ * 4 + y_)

    def at_x(x_):
        return dev(x_ % 2, z, c, x_ // 2, y)

    def at_y(y_):
        return dev(low, z, c, hi, y_)

    def at_g(low_, c_):
        return dev(low_, z, c_, hi, y)

    x_up, x_dn, x_far = (x + 1) % 4, (x + 3) % 4, (x + 2) % 4
    y_up, y_dn, y_far = (y + 1) % 4, (y + 3) % 4, (y + 2) % 4
    z_up = dev(low, (z + 1) % 8, c, hi, y)
    z_dn = dev(low, (z + 7) % 8, c, hi, y)
    twin = at_g(low, oc)
    group = [(low, oc), (olow, c), (olow, oc)]

    partners = [at_g(*m) for m in group] + [z_up, z_dn]
    partners += [at_y(y_up), at_y(y_dn), at_y(y_far)]
    partners += [dev(low, (z + 2) % 8, c, hi, y), dev(low, (z + 6) % 8, c, hi, y)]
    partners += [dev(low, z, c, 1 - hi, y), dev(olow, z, c, 1 - hi, y)]
    barrier = pltpu.get_barrier_semaphore()
    for partner in partners:
        pl.semaphore_signal(barrier, inc=1, device_id=partner, device_id_type=MESH)
    for kind in range(2):
        wkl[kind] = wkv[:, kind, :]
    pl.semaphore_wait(barrier, len(partners))

    drains = []

    def finish():
        for drain in drains:
            drain()

    def block_of(part, x_, y_, half=None):
        first, count = (0, 64) if half is None else (half * 32, 32)
        return xr.at[
            part, rows_of((x_ % 2) * 64 + first, count, 32),
            rows_of(((x_ // 2) * 4 + y_) * 640, 640, 128),
        ]

    prompts = Plane(
        lambda a, b, h=None: block_of(0, a, b, h), px, x, y, at_x, at_y,
        (xas.at[0], xar.at[0], xbs.at[0], xbr.at[0]),
    )
    answers = Plane(
        lambda a, b, h=None: block_of(1, b, a, h), rx, y, x, at_y, at_x,
        (xas.at[1], xar.at[1], xbs.at[1], xbr.at[1]),
    )
    planes = (prompts, answers)
    own0, own1 = block_of(0, x, y), block_of(1, x, y)

    group4 = [(low, c)] + group

    def piece(buf, z_, low_, c_):
        return buf.at[rows_of(low_ * 2560 + z_ * 320 + c_ * 160, 160, 32)]

    def wq_cols(low_, c_):
        return wq.at[:, rows_of((low_ * 2 + c_) * 256, 256, 256)]

    def wq_send(i):
        low_, c_ = group[i]
        return remote(
            wq_cols(low_, c_), piece(wqb, z, low, c), gs.at[i], gr.at[i], at_g(low_, c_)
        )

    def wk_cols(low_):
        return wkl.at[low_]

    def wk_send(i, low_):
        return remote(wk_cols(low_), piece(wkb, z, low, c), ks.at[i], kr.at[i], at_g(low_, 0))

    qring = Ring(
        lambda z_, p: piece(wqb, z_, *group4[p]), qrs, qrr, z, z_up, z_dn, 4
    )
    kring = Ring(
        lambda z_, p: piece(wkb, z_, *group4[p]), krs, krr, z, z_up, z_dn, 4
    )

    def if_keys(run):
        pl.when(c == 0)(run)

    prompts.send_a()
    prompts.send_b(0, px)

    @pl.when(c == 0)
    def _():
        kring.start(0, wk_cols(low))
        wk_send(1, olow).start()
        pltpu.make_async_copy(wk_cols(low), piece(wkb, z, low, c), loc.at[3]).start()

    @pl.when(c == 1)
    def _():
        wk_send(0, low).start()
        wk_send(2, olow).start()

    for i in range(3):
        wq_send(i).start()
    qring.start(0, wq_cols(low, c))
    answers.send_a()
    answers.send_b(0, rx)

    local0 = pltpu.make_async_copy(px, own0, loc.at[0])
    local1 = pltpu.make_async_copy(rx, own1, loc.at[1])
    local2 = pltpu.make_async_copy(wq_cols(low, c), piece(wqb, z, low, c), loc.at[2])
    local0.start()
    local1.start()
    local2.start()

    def wo_view(c_):
        return lambda z_, h: wob.at[rows_of(z_ * 320 + c_ * 160 + h * 80, 80, 16)]

    wo_own = wob.at[rows_of(z * 320 + c * 160, 160, 32)]
    local4 = pltpu.make_async_copy(wo, wo_own, loc.at[4])
    local4.start()

    oring = Ring(wo_view(c), ors, orr, z, z_up, z_dn)
    otwin = Twin(oring, wo_view(oc), ots, otr, twin)
    for h in range(2):
        oring.start(h, wo.at[pl.ds(h * 80, 80)])
    remote(wo, wo_own, o1.at[0], o1.at[1], twin).start()
    drains.append(lambda: remote(wo_own, wo_own, o1.at[0], o1.at[1], twin).wait_send())
    drains.append(oring.drain)
    drains.append(otwin.drain)

    @if_keys
    def _():
        for i in range(3):
            here = piece(wkb, z, *group[i])
            remote(here, here, ks.at[i], kr.at[i], twin).wait_recv()
            kring.start(i + 1)

    prompts.pass_a()
    prompts.pass_b(0)
    for i in range(3):
        here = piece(wqb, z, *group[i])
        remote(here, here, gs.at[i], gr.at[i], twin).wait_recv()
        qring.start(i + 1)
    prompts.pass_far()
    if_keys(lambda: kring.forward(1))
    answers.pass_a()
    qring.forward(1, parts=(0,))
    prompts.pass_b(1)
    prompts.pass_b(2)
    if_keys(lambda: kring.forward(2))
    prompts.pass_b(3)
    prompts.pass_b(4)
    answers.pass_b(0)
    answers.pass_far()
    qring.forward(1, parts=(1, 2, 3))
    if_keys(lambda: kring.forward(3))

    iota = lax.broadcasted_iota(jnp.int32, (32, 128), 0)
    for c_ in range(2):
        for low_ in range(2):
            for h in range(2):
                sid = spans[2 * (low_ * 16 + z * 2 + c_) + h]
                first = c_ * 128 + low_ * 64 + h * 32
                rpos[pl.ds(first, 32), :] = (sid * 32 + iota).astype(F32)
                rpos[pl.ds(256 + first, 32), :] = (2048 + c_ * 64 + h * 32 + iota).astype(F32)
    first_half = lax.broadcasted_iota(jnp.int32, (128, 128), 1) < 64

    @pl.loop(0, 4)
    def _(i):
        rows = rows_of(i * 128, 128, 128)
        angles = rpos[rows, :] * inv[...]
        cosb[rows, :] = jnp.cos(angles)
        sine = jnp.sin(angles)
        sinb[rows, :] = jnp.where(first_half, -sine, sine)

    for copy in (local0, local1, local2, local4):
        copy.wait()
    for j in range(5):
        prompts.end_b(j)

    drains.append(lambda: [drain() for plane in planes for drain in plane.drains])
    drains.append(qring.drain)
    drains.append(lambda: [wq_send(i).wait_send() for i in range(3)])

    def drain_keys():
        @pl.when(c == 0)
        def _():
            kring.drain()
            wk_send(1, olow).wait_send()

        @pl.when(c == 1)
        def _():
            wk_send(0, low).wait_send()
            wk_send(2, olow).wait_send()

    drains.append(drain_keys)

    def normed(c_, g):
        return nb.at[rows_of((g // 2) * 256 + c_ * 128 + (g % 2) * 64, 64, 64)]

    def norm_send(c_, g):
        return remote(normed(c_, g), normed(c_, g), nbs.at[g], nbr.at[g], twin)

    def norm(g):
        @pl.loop(0, 4)
        def _(i):
            rows = xr[g // 2, rows_of((g % 2) * 64 + i * 16, 16, 16), :].astype(F32)
            mean = jnp.mean(rows * rows, axis=-1, keepdims=True)
            first = (g // 2) * 256 + c * 128 + (g % 2) * 64 + i * 16
            nb[rows_of(first, 16, 16), :] = (
                rows * lax.rsqrt(mean + 1e-06) * gain[...]
            ).astype(BF)

        norm_send(c, g).start()

    drains.append(lambda: [norm_send(c, g).wait_send() for g in range(4)])
    norm(0)
    norm(1)
    if_keys(kring.last)
    if_keys(lambda: pltpu.make_async_copy(wk_cols(low), piece(wkb, z, low, c), loc.at[3]).wait())
    qring.forward(2, parts=(0,))
    for j in range(1, 5):
        answers.pass_b(j)
    for g in range(2):
        norm_send(oc, g).wait_recv()

    def head(values, gains, rows):
        mean = jnp.mean(values * values, axis=-1, keepdims=True)
        values = values * lax.rsqrt(mean + 1e-06) * gains[...]
        return values * cosb[rows, :] + pltpu.roll(values, 64, 1) * sinb[rows, :]

    def kv_send(i, p):
        low_, c_ = group[i]
        own = kvp.at[low, rows_of(z * 256, 256, 256)] if p == 0 else kvr.at[low]
        return remote(
            own, own, kvs.at[i, p], kvrv.at[0 if i == 0 else 1, p], at_g(low_, c_)
        )

    def keys(p):
        rows = pl.ds(p * 256, 256)
        acck[rows, :] = jnp.zeros((256, 128), F32)

        @pl.loop(0, 10)
        def _(i):
            part = rows_of(i * 512, 512, 512)
            acck[rows, :] += jnp.dot(nb[rows, part], wkb[part, :], preferred_element_type=F32)

        raw = acck[rows, :]
        mine = jnp.where(low == 0, head(raw, kg, rows), raw).astype(BF)
        if p == 0:
            kvp[low, rows_of(z * 256, 256, 256), :] = mine
        else:
            kvr[low] = mine
        for k in (1, 2, 0):
            kv_send(k, p).start()

    if_keys(lambda: keys(0))
    qring.forward(2, parts=(1, 2, 3))
    for j in range(5):
        answers.end_b(j)
    norm(2)
    norm(3)

    def drain_kv():
        @pl.when(c == 0)
        def _():
            for p in range(2):
                for i in range(3):
                    kv_send(i, p).wait_send()

    drains.append(drain_kv)

    def kv_wait(kind, i, p):
        part = kvp.at[kind, rows_of(z * 256, 256, 256)] if p == 0 else kvr.at[kind]
        remote(part, part, kvs.at[0, p], kvrv.at[i, p], twin).wait_recv()

    lane = lax.broadcasted_iota(jnp.int32, (8, 2048), 1)

    def key_positions(j, held):
        z_, c_, low_, h = j // 8, (j // 4) % 2, (j // 2) % 2, j % 2
        sid = spans[2 * (low_ * 16 + z_ * 2 + c_) + h]
        return jnp.where(lane // 32 == j, sid * 32 + lane % 32, held)

    kpos[...] = lax.fori_loop(
        0, 64, key_positions, jnp.zeros((8, 2048), jnp.int32)
    ).astype(F32)
    pl.when(c == 1)(lambda: kv_wait(low, 0, 0))
    kv_wait(olow, 1, 0)

    def kv_view(kind):
        def view(z_, h):
            first, count = (0, 256) if h is None else (h * 128, 128)
            return kvp.at[kind, rows_of(z_ * 256 + first, count, 128)]

        return view

    spread = Spread(
        kv_view(c), kv_view(oc), (vrs, vrr, vts, vtr), z,
        lambda z_: dev(low, z_, c, hi, y), twin,
    )
    spread.start()
    drains.append(spread.drain)
    qring.forward(3)
    oring.forward(1, otwin, (0,))
    for g in (2, 3):
        norm_send(oc, g).wait_recv()
    spread.middle()
    if_keys(lambda: keys(1))
    oring.forward(1, otwin, (1,))
    qring.last()
    accq[...] = jnp.zeros_like(accq)

    @pl.loop(0, 10)
    def _(i):
        part = rows_of(i * 512, 512, 512)
        accq[...] += jnp.dot(nb[:, part], wqb[part, :], preferred_element_type=F32)

    spread.last()
    for i in range(4):
        rows = pl.ds(i * 128, 128)
        for h in range(2):
            qb[i, pl.ds(h * 128, 128), :] = head(
                accq[rows, pl.ds(h * 128, 128)], qg, rows
            ).astype(BF)
    oring.forward(2, otwin)
    pl.when(c == 1)(lambda: kv_wait(low, 0, 1))
    kv_wait(olow, 1, 1)
    spread.twins()

    scale = 128 ** (-0.5)

    def attend(c_, p):
        queries = qb[p * 2 + c_]
        scores = lax.dot_general(queries, kvp[0], NT, preferred_element_type=F32) * scale
        if p == 0:
            mine = rpos[rows_of(c_ * 128, 128, 128), :][:, :1]
            allowed = kpos[:1, :] <= jnp.concatenate([mine, mine], axis=0)
            scores = jnp.where(allowed, scores, -1e30)
        peak = jnp.max(scores, axis=-1, keepdims=True)
        if p == 1:
            own = lax.dot_general(queries, kvr[0], NT, preferred_element_type=F32) * scale
            q_row = lax.broadcasted_iota(jnp.int32, (256, 256), 0) % 128
            k_row = lax.broadcasted_iota(jnp.int32, (256, 256), 1)
            allowed = ((q_row // 64) == ((k_row // 64) % 2)) & (
                (k_row // 128) * 64 + k_row % 64 <= c_ * 64 + q_row % 64
            )
            own = jnp.where(allowed, own, -1e30)
            peak = jnp.maximum(peak, jnp.max(own, axis=-1, keepdims=True))
        weights = jnp.exp(scores - peak)
        total = jnp.sum(weights, axis=-1, keepdims=True)
        summed = jnp.dot(weights.astype(BF), kvp[1], preferred_element_type=F32)
        if p == 1:
            more = jnp.exp(own - peak)
            total = total + jnp.sum(more, axis=-1, keepdims=True)
            summed = summed + jnp.dot(more.astype(BF), kvr[1], preferred_element_type=F32)
        result = (summed / total).astype(BF)
        for h in range(2):
            atts[c_, pl.ds(p * 128, 128), pl.ds(h * 128, 128)] = result[h * 128 : (h + 1) * 128]

    def att_cols(low_, c_):
        return attb.at[:, rows_of((low_ * 2 + c_) * 256, 256, 256)]

    def att_send(i):
        low_, c_ = group[i]
        return remote(atts.at[c_], att_cols(low, c), ats.at[i], atr.at[i], at_g(low_, c_))

    attend(oc, 0)
    attend(oc, 1)
    att_send(2).start()
    att_send(0).start()
    attend(c, 0)
    attend(c, 1)
    att_send(1).start()
    drains.append(lambda: [att_send(i).wait_send() for i in range(3)])
    attb[:, rows_of((low * 2 + c) * 256, 256, 256)] = atts[c]
    other_own = wob.at[rows_of(z * 320 + oc * 160, 160, 32)]
    remote(other_own, other_own, o1.at[0], o1.at[1], twin).wait_recv()
    otwin.wait_recv(range(2))
    for i in range(3):
        part = att_cols(*group[i])
        remote(part, part, ats.at[i], atr.at[i], twin).wait_recv()

    def y_send(k, p, y_):
        place = (y_ - y + 3) % 4
        rows = pl.ds(p * 128, 128)
        return remote(
            osend.at[k, rows], ry.at[place, rows], ys.at[k, p], yr.at[place, p], at_y(y_)
        )

    def y_of(k):
        return (z // 2 + (0, 3 + 2 * (z % 2), 5 - 2 * (z % 2), 2)[k]) % 4

    def project(k):
        y_ = y_of(k)
        weights = wob[rows_of(y_ * 640, 640, 128), :]
        for p in range(2):
            rows = pl.ds(p * 128, 128)
            osend[k, rows, :] = lax.dot_general(
                attb[rows, :], weights, NT, preferred_element_type=F32
            ).astype(BF)
            pl.when(y_ != y)(lambda: y_send(k, p, y_).start())

    def drain_y():
        for k in range(4):
            for p in range(2):
                pl.when(y_of(k) != y)(lambda k=k, p=p: y_send(k, p, y_of(k)).wait_send())

    drains.append(drain_y)
    project(0)
    project(1)
    oring.forward(3, otwin)
    otwin.wait_recv((2,))
    project(2)
    oring.last(otwin)
    otwin.wait_recv((3,))
    project(3)

    def x_send(low_, p):
        return remote(
            xs.at[pl.ds(p * 128 + low_ * 64, 64)], xrx.at[hi, p],
            zs.at[low_, p], zr.at[hi, p], dev(low_, z, c, low, y),
        )

    mine = (y - z // 2 + 4) % 4
    slot = jnp.where(mine == 2, 3, jnp.where(mine % 2 == 0, 0, 2 - (mine // 2 + z) % 2))
    for p in range(2):
        rows = pl.ds(p * 128, 128)
        total = osend[slot, rows, :].astype(F32)
        for i in range(3):
            part = ry.at[i, rows]
            remote(part, part, ys.at[0, p], yr.at[i, p], twin).wait_recv()
            total += ry[i, rows, :].astype(F32)
        xs[rows, :] = total.astype(BF)
        for low_ in range(2):
            here = jnp.logical_and(hi == low, low == low_)

            @pl.when(here)
            def _(low_=low_, p=p):
                xrx[hi, p] = xs[pl.ds(p * 128 + low_ * 64, 64), :]

            pl.when(jnp.logical_not(here))(lambda low_=low_, p=p: x_send(low_, p).start())

    offsets = c * 64 + lax.broadcasted_iota(jnp.int32, (64, 640), 0)
    for p in range(2):
        for hi_ in range(2):

            @pl.when(jnp.logical_not(jnp.logical_and(hi == low, hi == hi_)))
            def _(hi_=hi_, p=p):
                part = xrx.at[hi_, p]
                remote(part, part, zs.at[0, p], zr.at[hi_, p], twin).wait_recv()

        total = xrx[0, p].astype(F32) + xrx[1, p].astype(F32)
        if p == 0:
            po[...] = total.astype(BF)
        else:
            ro[...] = jnp.where(offsets < lens[ctx // 2], total, 0.0).astype(BF)

    finish()
    for low_ in range(2):
        here = jnp.logical_and(hi == low, low == low_)

        @pl.when(jnp.logical_not(here))
        def _(low_=low_):
            for p in range(2):
                x_send(low_, p).wait_send()


def body(prompt_x, resp_x, span_ids, lengths, in_gain, q_gain, k_gain, w_query, w_keyval, w_out):
    half = 1000000.0 ** (-(np.arange(64) * 2.0) / 128)
    inverse = np.concatenate([half, half])[None, :].astype(np.float32)
    dma = pltpu.SemaphoreType.DMA
    hbm, vmem, smem = (pl.BlockSpec(memory_space=s) for s in (pl.ANY, pltpu.VMEM, pltpu.SMEM))
    out = jax.ShapeDtypeStruct((64, 640), BF)
    return pl.pallas_call(
        kernel,
        out_shape=(out, out),
        in_specs=[smem, smem, hbm, hbm, vmem, vmem, vmem, vmem, hbm, vmem, hbm],
        out_specs=(vmem, vmem),
        scratch_shapes=[
            pltpu.VMEM((2, 128, 5120), BF),
            pltpu.VMEM((512, 5120), BF),
            pltpu.VMEM((5120, 256), BF),
            pltpu.VMEM((5120, 128), BF),
            pltpu.VMEM((2560, 1024), BF),
            pltpu.VMEM((2, 160, 128), BF),
            pltpu.VMEM((512, 256), F32),
            pltpu.VMEM((512, 128), F32),
            pltpu.VMEM((512, 128), F32),
            pltpu.VMEM((512, 128), F32),
            pltpu.VMEM((512, 128), F32),
            pltpu.VMEM((8, 2048), F32),
            pltpu.VMEM((4, 256, 128), BF),
            pltpu.VMEM((2, 2048, 128), BF),
            pltpu.VMEM((2, 256, 128), BF),
            pltpu.VMEM((2, 256, 256), BF),
            pltpu.VMEM((256, 1024), BF),
            pltpu.VMEM((4, 256, 640), BF),
            pltpu.VMEM((3, 256, 640), BF),
            pltpu.VMEM((256, 640), BF),
            pltpu.VMEM((2, 2, 64, 640), BF),
            dma((5,)),
            dma((2, 2, 2)), dma((2, 2, 2)),
            dma((2, 2, 2, 5)), dma((2, 2, 2, 5)),
            dma((3,)), dma((3,)),
            dma((3,)), dma((3,)),
            dma((2, 4, 4)), dma((2, 4, 4)),
            dma((2, 4, 4)), dma((2, 4, 4)),
            dma((2, 4, 2)), dma((2, 4, 2)),
            dma((2, 4, 2)), dma((2, 4, 2)),
            dma((2,)),
            dma((4,)), dma((4,)),
            dma((3, 2)), dma((2, 2)),
            dma((2, 4)), dma((2, 4)),
            dma((2, 4)), dma((2, 4)),
            dma((3,)), dma((3,)),
            dma((4, 2)), dma((3, 2)),
            dma((2, 2)), dma((2, 2)),
        ],
        compiler_params=pltpu.CompilerParams(
            collective_id=0, has_side_effects=True, vmem_limit_bytes=56 * 2**20
        ),
        name="attention_block",
    )(
        span_ids, lengths, prompt_x, resp_x, in_gain[None, :], q_gain[None, :], k_gain[None, :],
        inverse, w_query, w_keyval, jnp.transpose(w_out),
    )


def solution(mesh):
    placed = (
        P("ctx", "tp"),
        P("ctx", "tp"),
        P(),
        P(),
        P(),
        P(),
        P(),
        P("ctx", "tp"),
        P("ctx", None, "tp"),
        P("tp", "ctx"),
    )
    return jax.shard_map(
        body,
        mesh=mesh,
        in_specs=placed,
        out_specs=(P("ctx", "tp"), P("ctx", "tp")),
        check_vma=False,
    )
```

time: 329 us -> 112 us (0.34)
  blocking collectives: 143 us -> 0 us
  waiting for transfers between devices: 124 us -> 0 us
  Pallas kernels: 0 us -> 109 us
  matrix products: 22 us -> 0 us
  between operations: 14.3 us -> 0.65 us
  local copies, waits for them, and re-layouts: 11.8 us -> 2.2 us
  other arithmetic: 8.4 us -> 0 us
  starting transfers between devices: 4.76 us -> 0 us
    all_gather x4 -> x0, blocking collectives: 143 us -> none  [the longest x1 38.5 us: body(): lax.all_gather(resp_x, 'tp', axis=1, tiled=True)]
    pallas_call x0 -> x1, Pallas kernels: none -> 109 us  [body(): pl.pallas_call(kernel, out_shape=(out, out), in_specs=[smem, smem, hbm, h...]
    unnamed x5 -> x0, waiting for transfers between devices: 78.5 us -> none
    all_gather x3 -> x0, waiting for transfers between devices: 45 us -> none  [the longest x1 45 us: body(): lax.all_gather(w_out, 'ctx', axis=1, tiled=True)]
    dot_general x21 -> x0, matrix products: 22 us -> none  [the longest x1 7.54 us: body(): projected = jnp.dot(attended, out_w, preferred_element_type=jnp.float32)]
    reshape x1 -> x0, local copies, waits for them, and re-layouts: 5.94 us -> none  [body(): keyval_w.reshape(keyval_w.shape[0], -1)]
    reduce_sum x14 -> x0, other arithmetic: 5.17 us -> none  [the longest x9 3.11 us: softmax_update(): new_total = old_total * factor + jnp.sum(weights, axis=-1)]
    ppermute x2 -> x0, starting transfers between devices: 4.61 us -> none  [shifted(): return lax.ppermute(shard, axis, pairs)]
  transfers between devices with their start and end apart: 6 -> 0, of which waited for: 2 -> 0; matrix products, arithmetic and copies ran while one was open for 9% -> 0% of each run, Pallas kernels for 0% -> 0%
where the time goes in v1:
time: 112 us
  Pallas kernels  109 us (97%)
  local copies, waits for them, and re-layouts  2.2 us (2%)
    pallas_call x1, Pallas kernels, body(): pl.pallas_call(kernel, out_shape=(out, out), in_specs=[smem, smem, hbm, h...  109 us

profile of v1, /device:TPU:16, one launch (start us, length us, event | category | flops | bytes accessed | tf_op | source)
XLA Modules:
  0.0 112.0 jit_solution(16206731559552863809)
XLA Ops:
  0.6 109.1 %attention_block.1 = (bf16[64,640]{1,0:T(8,128)(2,1)}, bf16[64,640]{1,0:T(8,128)(2,1)}) custom-call(s32[64]{0:T(128)} %spans.1, s32[16]{0:T(128)} %lens.1, bf16[64,640]{1,0:T(8,128)(2,1)} %px.1, bf16[64,640]{1,0:T(8,128)(2,1)} %rx.1, f32[1,5120]{1,0:T(1,128)} %bitcast.5, f32[1,128]{1,0:T(1,128)} %bitcast.6, f32[1,128]{1,0:T(1,128)} %bitcast.7, ...), custom_call_target="tpu_custom_call" | custom-call | tf_op jit(solution)/shard_map/attention_block/pallas_call | solution.py:793
  109.7 0.0 copy-start
  109.8 1.6 %copy.15 = bf16[64,640]{1,0:T(8,128)(2,1)} copy(bf16[64,640]{1,0:T(8,128)(2,1)} %get-tuple-element.4) | data formatting | bytes 163840
  111.3 0.0 copy-done
  111.3 0.6 copy.16
Async XLA Ops:
  109.7 1.6 %copy-start = (bf16[64,640]{1,0:T(8,128)(2,1)S(1)}, bf16[64,640]{1,0:T(8,128)(2,1)}, u32[]{:S(2)}) copy-start(bf16[64,640]{1,0:T(8,128)(2,1)} %get-tuple-element.5) | copy-start | bytes 245764

commit v2 on v1

--- a/solution.py
+++ b/solution.py
@@ -146,8 +146,8 @@
 
 
 class Spread:
-    def __init__(self, view, other, sems, z, to_z, twin):
-        self.view, self.other, self.z, self.to_z, self.twin = view, other, z, to_z, twin
+    def __init__(self, view, others, sems, z, to_z, devs):
+        self.view, self.others, self.z, self.to_z, self.devs = view, others, z, to_z, devs
         self.send, self.recv, self.tsend, self.trecv = sems
 
     def make(self, way, k, sender):
@@ -161,11 +161,13 @@
             self.to_z((self.z + sign * hops + 8) % 8),
         )
 
-    def pair(self, way, k, view):
+    def pair(self, way, k, i, view):
         sign = 1 if way == 0 else -1
         block = (self.z - sign * (k + 1) + 16) % 8
         part = view(block, way if k == 3 else None)
-        return remote(part, part, self.tsend.at[way, k], self.trecv.at[way, k], self.twin)
+        return remote(
+            part, part, self.tsend.at[i, way, k], self.trecv.at[i, way, k], self.devs[i]
+        )
 
     def start(self):
         for k in (1, 0):
@@ -174,7 +176,8 @@
 
     def arrive(self, way, k):
         self.make(way, k, False).wait_recv()
-        self.pair(way, k, self.view).start()
+        for i in (1, 2, 0):
+            self.pair(way, k, i, self.view).start()
 
     def middle(self):
         for way in (0, 1):
@@ -192,13 +195,15 @@
     def twins(self):
         for k in range(4):
             for way in (0, 1):
-                self.pair(way, k, self.other).wait_recv()
+                for i in range(3):
+                    self.pair(way, k, i, self.others[i]).wait_recv()
 
     def drain(self):
         for k in range(4):
             for way in (0, 1):
                 self.make(way, k, True).wait_send()
-                self.pair(way, k, self.view).wait_send()
+                for i in range(3):
+                    self.pair(way, k, i, self.view).wait_send()
 
 
 class Plane:
@@ -606,16 +611,16 @@
     pl.when(c == 1)(lambda: kv_wait(low, 0, 0))
     kv_wait(olow, 1, 0)
 
-    def kv_view(kind):
+    def kv_view(low_, kind):
         def view(z_, h):
-            first, count = (0, 256) if h is None else (h * 128, 128)
-            return kvp.at[kind, rows_of(z_ * 256 + first, count, 128)]
+            first, count = (0, 128) if h is None else (h * 64, 64)
+            return kvp.at[kind, rows_of(z_ * 256 + low_ * 128 + first, count, 64)]
 
         return view
 
     spread = Spread(
-        kv_view(c), kv_view(oc), (vrs, vrr, vts, vtr), z,
-        lambda z_: dev(low, z_, c, hi, y), twin,
+        kv_view(low, c), [kv_view(*m) for m in group], (vrs, vrr, vts, vtr), z,
+        lambda z_: dev(low, z_, c, hi, y), [at_g(*m) for m in group],
     )
     spread.start()
     drains.append(spread.drain)
@@ -641,7 +646,6 @@
             qb[i, pl.ds(h * 128, 128), :] = head(
                 accq[rows, pl.ds(h * 128, 128)], qg, rows
             ).astype(BF)
-    oring.forward(2, otwin)
     pl.when(c == 1)(lambda: kv_wait(low, 0, 1))
     kv_wait(olow, 1, 1)
     spread.twins()
@@ -687,7 +691,9 @@
     attend(oc, 1)
     att_send(2).start()
     att_send(0).start()
+    oring.forward(2, otwin, (0,))
     attend(c, 0)
+    oring.forward(2, otwin, (1,))
     attend(c, 1)
     att_send(1).start()
     drains.append(lambda: [att_send(i).wait_send() for i in range(3)])
@@ -699,40 +705,50 @@
         part = att_cols(*group[i])
         remote(part, part, ats.at[i], atr.at[i], twin).wait_recv()
 
+    early, late = (1 - z % 2) * 384, (z % 2) * 256
+
+    def cols_of(k):
+        return pl.ds(0, 640) if k < 3 else (
+            rows_of(early, 256, 128) if k == 3 else rows_of(late, 384, 128)
+        )
+
     def y_send(k, p, y_):
         place = (y_ - y + 3) % 4
-        rows = pl.ds(p * 128, 128)
+        rows, cols = pl.ds(p * 128, 128), cols_of(k)
         return remote(
-            osend.at[k, rows], ry.at[place, rows], ys.at[k, p], yr.at[place, p], at_y(y_)
+            osend.at[min(k, 3), rows, cols], ry.at[place, rows, cols],
+            ys.at[k, p], yr.at[place, p, k // 4], at_y(y_),
         )
 
     def y_of(k):
-        return (z // 2 + (0, 3 + 2 * (z % 2), 5 - 2 * (z % 2), 2)[k]) % 4
+        return (z // 2 + (0, 3 + 2 * (z % 2), 5 - 2 * (z % 2), 2, 2)[k]) % 4
 
     def project(k):
         y_ = y_of(k)
-        weights = wob[rows_of(y_ * 640, 640, 128), :]
+        first = y_ * 640 + (0, 0, 0, early, late)[k]
+        weights = wob[rows_of(first, (640, 640, 640, 256, 384)[k], 128), :]
         for p in range(2):
             rows = pl.ds(p * 128, 128)
-            osend[k, rows, :] = lax.dot_general(
+            osend[min(k, 3), rows, cols_of(k)] = lax.dot_general(
                 attb[rows, :], weights, NT, preferred_element_type=F32
             ).astype(BF)
             pl.when(y_ != y)(lambda: y_send(k, p, y_).start())
 
     def drain_y():
-        for k in range(4):
+        for k in range(5):
             for p in range(2):
                 pl.when(y_of(k) != y)(lambda k=k, p=p: y_send(k, p, y_of(k)).wait_send())
 
     drains.append(drain_y)
     project(0)
+    oring.forward(3, otwin)
     project(1)
-    oring.forward(3, otwin)
     otwin.wait_recv((2,))
     project(2)
+    project(3)
     oring.last(otwin)
     otwin.wait_recv((3,))
-    project(3)
+    project(4)
 
     def x_send(low_, p):
         return remote(
@@ -744,10 +760,20 @@
     slot = jnp.where(mine == 2, 3, jnp.where(mine % 2 == 0, 0, 2 - (mine // 2 + z) % 2))
     for p in range(2):
         rows = pl.ds(p * 128, 128)
+
+        def y_wait(k, p=p):
+            for i in range(3):
+                part = ry.at[i, pl.ds(p * 128, 128), cols_of(k)]
+                remote(part, part, ys.at[0, p], yr.at[i, p, k // 4], twin).wait_recv()
+
+        @pl.when(mine == 2)
+        def _(y_wait=y_wait):
+            y_wait(3)
+            y_wait(4)
+
+        pl.when(mine != 2)(lambda: y_wait(0))
         total = osend[slot, rows, :].astype(F32)
         for i in range(3):
-            part = ry.at[i, rows]
-            remote(part, part, ys.at[0, p], yr.at[i, p], twin).wait_recv()
             total += ry[i, rows, :].astype(F32)
         xs[rows, :] = total.astype(BF)
         for low_ in range(2):
@@ -830,9 +856,9 @@
             dma((4,)), dma((4,)),
             dma((3, 2)), dma((2, 2)),
             dma((2, 4)), dma((2, 4)),
-            dma((2, 4)), dma((2, 4)),
+            dma((3, 2, 4)), dma((3, 2, 4)),
             dma((3,)), dma((3,)),
-            dma((4, 2)), dma((3, 2)),
+            dma((5, 2)), dma((3, 2, 2)),
             dma((2, 2)), dma((2, 2)),
         ],
         compiler_params=pltpu.CompilerParams(

time: 112 us -> 107 us (0.955)
  Pallas kernels: 109 us -> 104 us
    pallas_call x1, Pallas kernels: 109 us -> 104 us  [body(): pl.pallas_call(kernel, out_shape=(out, out), in_specs=[smem, smem, hbm, h...]
where the time goes in v2:
time: 107 us
  Pallas kernels  104 us (97%)
  local copies, waits for them, and re-layouts  2.2 us (2%)
    pallas_call x1, Pallas kernels, body(): pl.pallas_call(kernel, out_shape=(out, out), in_specs=[smem, smem, hbm, h...  104 us
    unnamed x4, local copies, waits for them, and re-layouts  2.2 us

profile of v2, /device:TPU:16, one launch (start us, length us, event | category | flops | bytes accessed | tf_op | source)
XLA Modules:
  0.0 106.9 jit_solution(13048292556821089647)
XLA Ops:
  0.6 104.1 %attention_block.1 = (bf16[64,640]{1,0:T(8,128)(2,1)}, bf16[64,640]{1,0:T(8,128)(2,1)}) custom-call(s32[64]{0:T(128)} %spans.1, s32[16]{0:T(128)} %lens.1, bf16[64,640]{1,0:T(8,128)(2,1)} %px.1, bf16[64,640]{1,0:T(8,128)(2,1)} %rx.1, f32[1,5120]{1,0:T(1,128)} %bitcast.5, f32[1,128]{1,0:T(1,128)} %bitcast.6, f32[1,128]{1,0:T(1,128)} %bitcast.7, ...), custom_call_target="tpu_custom_call" | custom-call | tf_op jit(solution)/shard_map/attention_block/pallas_call | solution.py:819
  104.7 0.0 copy-start
  104.7 1.6 %copy.15 = bf16[64,640]{1,0:T(8,128)(2,1)} copy(bf16[64,640]{1,0:T(8,128)(2,1)} %get-tuple-element.4) | data formatting | bytes 163840
  106.3 0.0 copy-done
  106.3 0.6 copy.16
Async XLA Ops:
  104.7 1.6 %copy-start = (bf16[64,640]{1,0:T(8,128)(2,1)S(1)}, bf16[64,640]{1,0:T(8,128)(2,1)}, u32[]{:S(2)}) copy-start(bf16[64,640]{1,0:T(8,128)(2,1)} %get-tuple-element.5) | copy-start | bytes 245764

commit v3 on v2

--- a/solution.py
+++ b/solution.py
@@ -313,7 +313,7 @@
 
 def kernel(
     spans, lens, px, rx, gain, qg, kg, inv, wq, wkv, wo,
-    po, ro,
+    both,
     xr, nb, wqb, wkb, wob, wkl, accq, acck, cosb, sinb, rpos, kpos, qb, kvp, kvr, atts, attb,
     osend, ry, xs, xrx,
     loc, xas, xar, xbs, xbr, gs, gr, ks, kr, qrs, qrr, krs, krr, ors, orr, ots, otr, o1,
@@ -629,8 +629,8 @@
     for g in (2, 3):
         norm_send(oc, g).wait_recv()
     spread.middle()
+    oring.forward(1, otwin, (1,))
     if_keys(lambda: keys(1))
-    oring.forward(1, otwin, (1,))
     qring.last()
     accq[...] = jnp.zeros_like(accq)
 
@@ -640,6 +640,7 @@
         accq[...] += jnp.dot(nb[:, part], wqb[part, :], preferred_element_type=F32)
 
     spread.last()
+    oring.forward(2, otwin, (0,))
     for i in range(4):
         rows = pl.ds(i * 128, 128)
         for h in range(2):
@@ -687,15 +688,15 @@
         low_, c_ = group[i]
         return remote(atts.at[c_], att_cols(low, c), ats.at[i], atr.at[i], at_g(low_, c_))
 
+    oring.forward(2, otwin, (1,))
     attend(oc, 0)
     attend(oc, 1)
     att_send(2).start()
     att_send(0).start()
-    oring.forward(2, otwin, (0,))
     attend(c, 0)
-    oring.forward(2, otwin, (1,))
     attend(c, 1)
     att_send(1).start()
+    oring.forward(3, otwin)
     drains.append(lambda: [att_send(i).wait_send() for i in range(3)])
     attb[:, rows_of((low * 2 + c) * 256, 256, 256)] = atts[c]
     other_own = wob.at[rows_of(z * 320 + oc * 160, 160, 32)]
@@ -727,12 +728,11 @@
         y_ = y_of(k)
         first = y_ * 640 + (0, 0, 0, early, late)[k]
         weights = wob[rows_of(first, (640, 640, 640, 256, 384)[k], 128), :]
+        osend[min(k, 3), :, cols_of(k)] = lax.dot_general(
+            attb[...], weights, NT, preferred_element_type=F32
+        ).astype(BF)
         for p in range(2):
-            rows = pl.ds(p * 128, 128)
-            osend[min(k, 3), rows, cols_of(k)] = lax.dot_general(
-                attb[rows, :], weights, NT, preferred_element_type=F32
-            ).astype(BF)
-            pl.when(y_ != y)(lambda: y_send(k, p, y_).start())
+            pl.when(y_ != y)(lambda p=p: y_send(k, p, y_).start())
 
     def drain_y():
         for k in range(5):
@@ -741,7 +741,6 @@
 
     drains.append(drain_y)
     project(0)
-    oring.forward(3, otwin)
     project(1)
     otwin.wait_recv((2,))
     project(2)
@@ -796,9 +795,9 @@
 
         total = xrx[0, p].astype(F32) + xrx[1, p].astype(F32)
         if p == 0:
-            po[...] = total.astype(BF)
+            both[pl.ds(0, 64), :] = total.astype(BF)
         else:
-            ro[...] = jnp.where(offsets < lens[ctx // 2], total, 0.0).astype(BF)
+            both[pl.ds(64, 64), :] = jnp.where(offsets < lens[ctx // 2], total, 0.0).astype(BF)
 
     finish()
     for low_ in range(2):
@@ -815,12 +814,12 @@
     inverse = np.concatenate([half, half])[None, :].astype(np.float32)
     dma = pltpu.SemaphoreType.DMA
     hbm, vmem, smem = (pl.BlockSpec(memory_space=s) for s in (pl.ANY, pltpu.VMEM, pltpu.SMEM))
-    out = jax.ShapeDtypeStruct((64, 640), BF)
-    return pl.pallas_call(
+    out = jax.ShapeDtypeStruct((128, 640), BF)
+    both = pl.pallas_call(
         kernel,
-        out_shape=(out, out),
+        out_shape=out,
         in_specs=[smem, smem, hbm, hbm, vmem, vmem, vmem, vmem, hbm, vmem, hbm],
-        out_specs=(vmem, vmem),
+        out_specs=vmem,
         scratch_shapes=[
             pltpu.VMEM((2, 128, 5120), BF),
             pltpu.VMEM((512, 5120), BF),
@@ -869,6 +868,7 @@
         span_ids, lengths, prompt_x, resp_x, in_gain[None, :], q_gain[None, :], k_gain[None, :],
         inverse, w_query, w_keyval, jnp.transpose(w_out),
     )
+    return both[:64], both[64:]
 
 
 def solution(mesh):

time: 107 us -> 105 us (0.981)
  Pallas kernels: 104 us -> 102 us
    unnamed x4 -> x0, local copies, waits for them, and re-layouts: 2.2 us -> none
    pallas_call x1, Pallas kernels: 104 us -> 102 us  [body(): pl.pallas_call(kernel, out_shape=out, in_specs=[smem, smem, hbm, hbm, vme...]
    slice x0 -> x1, local copies, waits for them, and re-layouts: none -> 1.61 us  [body(): return (both[:64], both[64:])]
where the time goes in v3:
time: 105 us
  Pallas kernels  102 us (97%)
  local copies, waits for them, and re-layouts  1.61 us (2%)
    pallas_call x1, Pallas kernels, body(): pl.pallas_call(kernel, out_shape=out, in_specs=[smem, smem, hbm, hbm, vme...  102 us

profile of v3, /device:TPU:16, one launch (start us, length us, event | category | flops | bytes accessed | tf_op | source)
XLA Modules:
  0.0 104.6 jit_solution(17121146603318448897)
XLA Ops:
  0.6 102.4 %attention_block.1 = bf16[128,640]{1,0:T(8,128)(2,1)} custom-call(s32[64]{0:T(128)} %spans.1, s32[16]{0:T(128)} %lens.1, bf16[64,640]{1,0:T(8,128)(2,1)} %px.1, bf16[64,640]{1,0:T(8,128)(2,1)} %rx.1, f32[1,5120]{1,0:T(1,128)} %bitcast.5, f32[1,128]{1,0:T(1,128)} %bitcast.6, f32[1,128]{1,0:T(1,128)} %bitcast.7, f32[1,128]{1,0:T(1,128)} %constant.2.clone.inv, ...), custom_call_target="tpu_custom_call" | custom-call | tf_op jit(solution)/shard_map/attention_block/pallas_call | solution.py:818
  103.0 1.6 %fusion = (bf16[64,640]{1,0:T(8,128)(2,1)}, bf16[64,640]{1,0:T(8,128)(2,1)}) fusion(bf16[128,640]{1,0:T(8,128)(2,1)} %attention_block.1), kind=kLoop, calls=%fused_computation | loop fusion | bytes 327680 | tf_op jit(solution)/shard_map/slice | solution.py:871

commit v4 on v3

--- a/solution.py
+++ b/solution.py
@@ -625,13 +625,14 @@
     spread.start()
     drains.append(spread.drain)
     qring.forward(3)
-    oring.forward(1, otwin, (0,))
     for g in (2, 3):
         norm_send(oc, g).wait_recv()
     spread.middle()
+    oring.forward(1, otwin, (0,))
     oring.forward(1, otwin, (1,))
     if_keys(lambda: keys(1))
     qring.last()
+    spread.last()
     accq[...] = jnp.zeros_like(accq)
 
     @pl.loop(0, 10)
@@ -639,7 +640,6 @@
         part = rows_of(i * 512, 512, 512)
         accq[...] += jnp.dot(nb[:, part], wqb[part, :], preferred_element_type=F32)
 
-    spread.last()
     oring.forward(2, otwin, (0,))
     for i in range(4):
         rows = pl.ds(i * 128, 128)

time: 105 us -> 102 us (0.971)
  Pallas kernels: 102 us -> 100 us
    pallas_call x1, Pallas kernels: 102 us -> 100 us  [body(): pl.pallas_call(kernel, out_shape=out, in_specs=[smem, smem, hbm, hbm, vme...]
where the time goes in v4:
time: 102 us
  Pallas kernels  100 us (98%)
  local copies, waits for them, and re-layouts  1.61 us (2%)
    pallas_call x1, Pallas kernels, body(): pl.pallas_call(kernel, out_shape=out, in_specs=[smem, smem, hbm, hbm, vme...  100 us

profile of v4, /device:TPU:16, one launch (start us, length us, event | category | flops | bytes accessed | tf_op | source)
XLA Modules:
  0.0 102.2 jit_solution(12310431801197146237)
XLA Ops:
  0.6 100.0 %attention_block.1 = bf16[128,640]{1,0:T(8,128)(2,1)} custom-call(s32[64]{0:T(128)} %spans.1, s32[16]{0:T(128)} %lens.1, bf16[64,640]{1,0:T(8,128)(2,1)} %px.1, bf16[64,640]{1,0:T(8,128)(2,1)} %rx.1, f32[1,5120]{1,0:T(1,128)} %bitcast.5, f32[1,128]{1,0:T(1,128)} %bitcast.6, f32[1,128]{1,0:T(1,128)} %bitcast.7, f32[1,128]{1,0:T(1,128)} %constant.2.clone.inv, ...), custom_call_target="tpu_custom_call" | custom-call | tf_op jit(solution)/shard_map/attention_block/pallas_call | solution.py:818
  100.6 1.6 %fusion = (bf16[64,640]{1,0:T(8,128)(2,1)}, bf16[64,640]{1,0:T(8,128)(2,1)}) fusion(bf16[128,640]{1,0:T(8,128)(2,1)} %attention_block.1), kind=kLoop, calls=%fused_computation | loop fusion | bytes 327680 | tf_op jit(solution)/shard_map/slice | solution.py:871

commit v5 on v4

--- a/solution.py
+++ b/solution.py
@@ -598,16 +598,6 @@
         part = kvp.at[kind, rows_of(z * 256, 256, 256)] if p == 0 else kvr.at[kind]
         remote(part, part, kvs.at[0, p], kvrv.at[i, p], twin).wait_recv()
 
-    lane = lax.broadcasted_iota(jnp.int32, (8, 2048), 1)
-
-    def key_positions(j, held):
-        z_, c_, low_, h = j // 8, (j // 4) % 2, (j // 2) % 2, j % 2
-        sid = spans[2 * (low_ * 16 + z_ * 2 + c_) + h]
-        return jnp.where(lane // 32 == j, sid * 32 + lane % 32, held)
-
-    kpos[...] = lax.fori_loop(
-        0, 64, key_positions, jnp.zeros((8, 2048), jnp.int32)
-    ).astype(F32)
     pl.when(c == 1)(lambda: kv_wait(low, 0, 0))
     kv_wait(olow, 1, 0)
 
@@ -624,6 +614,16 @@
     )
     spread.start()
     drains.append(spread.drain)
+    lane = lax.broadcasted_iota(jnp.int32, (8, 2048), 1)
+
+    def key_positions(j, held):
+        z_, c_, low_, h = j // 8, (j // 4) % 2, (j // 2) % 2, j % 2
+        sid = spans[2 * (low_ * 16 + z_ * 2 + c_) + h]
+        return jnp.where(lane // 32 == j, sid * 32 + lane % 32, held)
+
+    kpos[...] = lax.fori_loop(
+        0, 64, key_positions, jnp.zeros((8, 2048), jnp.int32)
+    ).astype(F32)
     qring.forward(3)
     for g in (2, 3):
         norm_send(oc, g).wait_recv()

time: 102 us -> 103 us (level)
  no operation moved by 1% of the time
where the time goes in v5:
time: 103 us
  Pallas kernels  101 us (98%)
  local copies, waits for them, and re-layouts  1.61 us (2%)
    pallas_call x1, Pallas kernels, body(): pl.pallas_call(kernel, out_shape=out, in_specs=[smem, smem, hbm, hbm, vme...  101 us

profile of v5, /device:TPU:16, one launch (start us, length us, event | category | flops | bytes accessed | tf_op | source)
XLA Modules:
  0.0 102.9 jit_solution(5653601634398294504)
XLA Ops:
  0.6 100.6 %attention_block.1 = bf16[128,640]{1,0:T(8,128)(2,1)} custom-call(s32[64]{0:T(128)} %spans.1, s32[16]{0:T(128)} %lens.1, bf16[64,640]{1,0:T(8,128)(2,1)} %px.1, bf16[64,640]{1,0:T(8,128)(2,1)} %rx.1, f32[1,5120]{1,0:T(1,128)} %bitcast.5, f32[1,128]{1,0:T(1,128)} %bitcast.6, f32[1,128]{1,0:T(1,128)} %bitcast.7, f32[1,128]{1,0:T(1,128)} %constant.2.clone.inv, ...), custom_call_target="tpu_custom_call" | custom-call | tf_op jit(solution)/shard_map/attention_block/pallas_call | solution.py:818
  101.3 1.6 %fusion = (bf16[64,640]{1,0:T(8,128)(2,1)}, bf16[64,640]{1,0:T(8,128)(2,1)}) fusion(bf16[128,640]{1,0:T(8,128)(2,1)} %attention_block.1), kind=kLoop, calls=%fused_computation | loop fusion | bytes 327680 | tf_op jit(solution)/shard_map/slice | solution.py:871
